TPU v7x, 32 devices: a whole 2x2x4 slice. The times are simulated.
32 devices in a mesh: site: 4 (over z), patch: 8 (over y, x, core).
Axes of the slice: x: 2, y: 2, z: 4, core: 2. Of those that a mesh axis runs over, the one named last changes fastest.
Arguments:
- slip_rates: bfloat16 [128, 64, 256], P('patch', 'site'), may hold values from -6 to 6
- green_tiles: bfloat16 [4, 256, 2, 1024], P('site', 'patch'), may hold values from -0.03125 to 0.03125
- patch_slot: int32 [128], replicated, may hold values from 0 to 255, as said below
Outputs:
- seismograms: float32 [4, 64, 2, 1280], P('site', 'patch')
Inputs may be any that keep to these rules, and one draw needn't show every extreme that they name: The values of patch_slot all differ. Patch p belongs to owner patch_slot[p] // 32 and fills its slot patch_slot[p] % 32; each owner has 1 to 32 patches in its first slots, and some owner has exactly 32. The 16 patches p with the same p // 16 include at most 4 of any one owner, and some such group includes exactly 4 of one owner.
All inputs are finite; a program needn't handle non-finite values.
Results may differ from a plain program's by a relative error of at most 0.0003.
Values may be sent and summed in bfloat16 or wider, within the bound.
No kernel may reach another device: no remote copies, remote signals or barrier semaphores. Data moves between devices by JAX's collectives and lax.ppermute only.
A program may use at most 64 MiB of HBM per device.

v0:
```python
import math

import jax
import jax.numpy as jnp
from jax import lax
from jax.sharding import PartitionSpec as P


def band_matrix(greens, samples):
    half_len = samples // 2
    lag_count = greens.shape[-1]
    length = samples + lag_count
    period = length + samples
    padded = jnp.pad(greens, ((0, 0), (0, 0), (half_len, period - half_len - lag_count)))
    repeated = jnp.tile(padded, (1, 1, half_len))
    shifted = repeated[..., : half_len * (period - 1)].reshape(
        greens.shape[0], greens.shape[1], half_len, period - 1
    )
    return shifted[..., : length + half_len]


def convolve_rows(slot_slips, kernels, row_count):
    item_count = slot_slips.shape[0]
    samples = slot_slips.shape[2]
    lag_count = kernels.shape[2]
    half_len = samples // 2
    length = samples + lag_count
    group_size = math.gcd(item_count, 8)
    blocks = item_count // group_size
    selected = slot_slips
    selected = selected.reshape(blocks, group_size, row_count, samples)
    kernel_blocks = kernels.reshape(blocks, group_size, 2, lag_count)

    def accumulate(running, operands):
        slip_block, kernel = operands
        band_rows = band_matrix(kernel, samples)
        running = running + jnp.einsum(
            "pvq,pcqt->vct",
            slip_block[..., :half_len],
            band_rows[..., half_len : half_len + length],
            preferred_element_type=jnp.float32,
        )
        running = running + jnp.einsum(
            "pvq,pcqt->vct",
            slip_block[..., half_len:],
            band_rows[..., :length],
            preferred_element_type=jnp.float32,
        )
        return (running, None)

    running, unused = lax.scan(
        accumulate, jnp.zeros((row_count, 2, length), jnp.float32), (selected, kernel_blocks)
    )
    return running


def route_tables(patch_slot, slot_width, sources, per_source, capacity, owner_now):
    owner_of = patch_slot // slot_width
    within = patch_slot % slot_width
    owners = owner_of.reshape(sources, per_source)
    same_owner = owners[:, :, None] == owners[:, None, :]
    earlier = lax.broadcasted_iota(jnp.int32, (per_source, per_source), 1) < lax.broadcasted_iota(
        jnp.int32, (per_source, per_source), 0
    )
    rank_of = jnp.sum((same_owner & earlier[None]).astype(jnp.int32), axis=2)
    source_code = (
        lax.broadcasted_iota(jnp.int32, (sources, per_source), 0) * capacity + rank_of
    ).reshape(-1)
    owner_code = owners * capacity + rank_of
    is_mine = owner_of == owner_now
    slot_index = lax.broadcasted_iota(jnp.int32, (slot_width, 1), 0)
    code_index = lax.broadcasted_iota(jnp.int32, (1, sources * capacity), 1)
    slot_pick = ((within[None, :] == slot_index) & is_mine[None, :]).astype(jnp.bfloat16)
    code_pick = (source_code[:, None] == code_index).astype(jnp.bfloat16)
    inbound = jnp.dot(slot_pick, code_pick, preferred_element_type=jnp.float32).astype(jnp.bfloat16)
    my_codes = lax.dynamic_index_in_dim(owner_code, owner_now, 0, keepdims=False)
    outbound = (code_index.reshape(-1, 1) == my_codes[None, :]).astype(jnp.bfloat16)
    return (inbound, outbound)


def local(slip_rates, green_tiles, patch_slot):
    sources = lax.axis_size("patch")
    per_source = slip_rates.shape[0]
    slot_width = green_tiles.shape[1]
    lag_count = green_tiles.shape[3]
    capacity = 2 * max(1, per_source // sources)
    own_index = lax.axis_index("patch")
    inbound, outbound = route_tables(
        patch_slot, slot_width, sources, per_source, capacity, own_index
    )
    gathered = lax.all_gather(slip_rates, "site", axis=1, tiled=True)
    resident = green_tiles[0].reshape(slot_width, 2 * lag_count)
    outgoing = jnp.dot(inbound.T, resident, preferred_element_type=jnp.float32).astype(jnp.bfloat16)
    outgoing = outgoing.reshape(sources, capacity, 2 * lag_count)
    arrived = lax.all_to_all(outgoing, "patch", split_axis=0, concat_axis=0, tiled=True)
    kernels = jnp.dot(
        outbound.T,
        arrived.reshape(sources * capacity, 2 * lag_count),
        preferred_element_type=jnp.float32,
    )
    kernels = kernels.astype(jnp.bfloat16).reshape(per_source, 2, lag_count)
    own_rows = gathered.shape[1] // sources
    result = lax.psum_scatter(
        convolve_rows(gathered, kernels, own_rows * lax.axis_size("patch")),
        "patch",
        scatter_dimension=0,
        tiled=True,
    )
    return result[None]


def solution(mesh):
    in_specs = (P("patch", "site", None), P("site", "patch", None, None), P())
    out_specs = P("site", "patch", None, None)
    return jax.shard_map(local, mesh=mesh, in_specs=in_specs, out_specs=out_specs, check_vma=False)
```

profile of v0, /device:TPU:0, one launch (start us, length us, event | category | flops | bytes accessed | tf_op | source)
XLA Modules:
  0.0 147.7 jit_solution(605371613801282635)
XLA Ops:
  6.5 0.7 and_select_fusion
  7.2 0.7 broadcast_compare_fusion
  7.9 0.1 reshape.46
  8.0 0.3 convert_reduce_fusion
  8.2 0.1 multiply_add_fusion
  8.3 0.1 add.50
  8.4 0.9 copy.10
  9.3 0.4 convolution_convert_fusion
  9.8 0.7 reshape.47
  10.5 5.2 %all-to-all-start = ((bf16[8,4,2048]{2,1,0:T(4,128)(2,1)}), bf16[8,4,2048]{2,1,0:T(4,128)(2,1)S(1)}, u32[]{:S(2)}, u32[]{:S(2)}) async-start(bf16[8,4,2048]{2,1,0:T(4,128)(2,1)} %reshape.47), calls=%async_computation | async-start | bytes 262144 | tf_op jit(solution)/shard_map/all_to_all | solution.py:95
  15.6 0.0 all-reduce.4.cloned.1.call-start
  15.7 16.7 %all_gather.3 = bf16[16,64,256]{2,1,0:T(8,128)(2,1)S(1)} all-gather(bf16[16,16,256]{2,1,0:T(8,128)(2,1)} %param.5), channel_id=1, replica_groups=mesh['site'=4,'patch'=8] {'site'}, dimensions={1}, use_global_device_ids=true | all-gather | bytes 655360 | tf_op jit(solution)/shard_map/all_gather | solution.py:91
  32.4 0.0 all-to-all-done
  32.4 0.2 convolution_convert_fusion.1
  32.6 0.0 copy-start
  32.6 48.4 %while.13 = (s32[]{:T(128)}, f32[64,2,1280]{2,0,1:T(8,128)S(1)}, bf16[2,8,64,256]{3,2,1,0:T(8,128)(2,1)S(1)}, bf16[2,8,2,1024]{3,1,2,0:T(8,128)(2,1)S(1)}, s32[]{:T(128)}, /*index=5*/bf16[]{:T(256)}, s32[]{:T(128)}) while((s32[]{:T(128)}, f32[64,2,1280]{2,0,1:T(8,128)S(1)}, bf16[2,8,64,256]{3,2,1,0:T(8,128)(2,1)S(1)}, ...), condition=%wide.region_2.3_spmd.clone, body=%wide.region_1.2_spmd.clone.sunk | while | flops 671580160 | bytes 45531232 | solution.py:51
  32.7 0.4 tile.15
  33.1 2.9 %slice.68 = bf16[8,2,196480]{2,0,1:T(8,128)(2,1)} slice(bf16[8,2,196608]{2,0,1:T(8,128)(2,1)S(1)} %bitcast.49), slice={[0:8], [0:2], [0:196480]} | slice | bytes 12574720 | tf_op jit(solution)/shard_map/while/body/eval_jaxpr/slice | solution.py:16
  36.0 13.6 %reshape.56 = bf16[8,2,128,1535]{3,2,0,1:T(8,128)(2,1)} reshape(bf16[8,2,196480]{2,0,1:T(8,128)(2,1)} %slice.68) | data formatting | bytes 12574720 | tf_op jit(solution)/shard_map/while/body/eval_jaxpr/reshape | solution.py:16
  49.7 3.5 %fusion.34 = f32[64,2,1280]{2,0,1:T(8,128)S(1)} fusion(bf16[8,2,128,1535]{3,2,0,1:T(8,128)(2,1)} %reshape.56, bf16[8,64,256]{2,1,0:T(8,128)(2,1)S(1)} %dynamic-slice_bitcast_fusion.7), kind=kOutput, calls=%fused_computation.7.clone.1 | convolution fusion | flops 335544320 | bytes 6029312 | tf_op jit(solution)/shard_map/while/body/eval_jaxpr/pvq,pcqt->vct/dot_general | solution.py:43
  53.2 3.7 %fusion.35 = f32[64,2,1280]{2,0,1:T(8,128)S(1)} fusion(f32[64,2,1280]{2,0,1:T(8,128)S(1)} %fusion.34, bf16[8,2,128,1535]{3,2,0,1:T(8,128)(2,1)} %reshape.56, f32[64,2,1280]{2,0,1:T(8,128)S(1)} %get-tuple-element.119, pred[]{:T(512)S(6)} %compare.7, bf16[8,64,256]{2,1,0:T(8,128)(2,1)S(1)} %dynamic-slice_bitcast_fusion.7), kind=kOutput, calls=%fused_computation.6.clone.1 | convolution fusion | flops 336035840 | bytes 7340033 | tf_op jit(solution)/shard_map/while/body/eval_jaxpr/pvq,pcqt->vct/dot_general | solution.py:37
  56.9 0.4 tile.15
  57.3 2.9 %slice.68 = bf16[8,2,196480]{2,0,1:T(8,128)(2,1)} slice(bf16[8,2,196608]{2,0,1:T(8,128)(2,1)S(1)} %bitcast.49), slice={[0:8], [0:2], [0:196480]} | slice | bytes 12574720 | tf_op jit(solution)/shard_map/while/body/eval_jaxpr/slice | solution.py:16
  60.2 13.6 %reshape.56 = bf16[8,2,128,1535]{3,2,0,1:T(8,128)(2,1)} reshape(bf16[8,2,196480]{2,0,1:T(8,128)(2,1)} %slice.68) | data formatting | bytes 12574720 | tf_op jit(solution)/shard_map/while/body/eval_jaxpr/reshape | solution.py:16
  73.9 3.5 %fusion.34 = f32[64,2,1280]{2,0,1:T(8,128)S(1)} fusion(bf16[8,2,128,1535]{3,2,0,1:T(8,128)(2,1)} %reshape.56, bf16[8,64,256]{2,1,0:T(8,128)(2,1)S(1)} %dynamic-slice_bitcast_fusion.7), kind=kOutput, calls=%fused_computation.7.clone.1 | convolution fusion | flops 335544320 | bytes 6029312 | tf_op jit(solution)/shard_map/while/body/eval_jaxpr/pvq,pcqt->vct/dot_general | solution.py:43
  77.4 3.7 %fusion.35 = f32[64,2,1280]{2,0,1:T(8,128)S(1)} fusion(f32[64,2,1280]{2,0,1:T(8,128)S(1)} %fusion.34, bf16[8,2,128,1535]{3,2,0,1:T(8,128)(2,1)} %reshape.56, f32[64,2,1280]{2,0,1:T(8,128)S(1)} %get-tuple-element.119, pred[]{:T(512)S(6)} %compare.7, bf16[8,64,256]{2,1,0:T(8,128)(2,1)S(1)} %dynamic-slice_bitcast_fusion.7), kind=kOutput, calls=%fused_computation.6.clone.1 | convolution fusion | flops 336035840 | bytes 7340033 | tf_op jit(solution)/shard_map/while/body/eval_jaxpr/pvq,pcqt->vct/dot_general | solution.py:37
  81.1 1.3 copy.7
  82.4 0.0 all-reduce.4.cloned.1.call-update
  82.4 0.0 copy-done
  82.5 0.6 dynamic-slice
  83.7 55.6 %all-reduce.4.cloned.1.call-done = f32[64,2,1280]{2,1,0:T(2,128)} async-done(((f32[64,2,1280]{2,1,0:T(2,128)}), f32[64,2,1280]{2,1,0:T(2,128)}) %all-reduce.4.cloned.1.call-update) | async-done | bytes 655376
  139.3 1.5 %dynamic-slice_bitcast_fusion.2 = f32[1,8,2,1280]{3,2,1,0:T(2,128)} fusion(f32[64,2,1280]{2,1,0:T(2,128)} %all-reduce.4.cloned.1.call-done, u32[]{:T(128)S(6)} %multiply.1), kind=kLoop, calls=%fused_computation.15 | loop fusion | bytes 163844 | tf_op jit(solution)/shard_map/broadcast_in_dim | solution.py:109
  (11 shorter events, 0.1 us)
Async XLA Ops:
  10.5 21.9 %all-to-all-start = ((bf16[8,4,2048]{2,1,0:T(4,128)(2,1)}), bf16[8,4,2048]{2,1,0:T(4,128)(2,1)S(1)}, u32[]{:S(2)}, u32[]{:S(2)}) async-start(bf16[8,4,2048]{2,1,0:T(4,128)(2,1)} %reshape.47), calls=%async_computation | async-start | bytes 262144 | tf_op jit(solution)/shard_map/all_to_all | solution.py:95
  15.6 123.6 %all-reduce.4.cloned.1.call-start = ((), (), s32[]{:S(2)}) async-start(), calls=%async_computation.1 | async-start | bytes 1310720
  32.6 49.8 %copy-start = (u32[32]{0:T(128)S(1)}, u32[32]{0:T(128)}, u32[]{:S(2)}) copy-start(u32[32]{0:T(128)} %constant.69) | copy-start | bytes 388
Sparse Core Ops, SparseCore 0:
  82.6 56.6 all-reduce.3
where the time goes:
time: 148 us
  waiting for transfers between devices  55.6 us (38%)
  local copies, waits for them, and re-layouts  39.3 us (27%)
  blocking collectives  16.7 us (11%)
  matrix products  15 us (10%)
  between operations  14.1 us (10%)
  starting transfers between devices  5.21 us (4%)
  other arithmetic  1.7 us (1%)
    unnamed x2, waiting for transfers between devices  55.6 us
    reshape x2, local copies, waits for them, and re-layouts, band_matrix(): repeated[..., :half_len * (period - 1)]  27.3 us
    all_gather x1, blocking collectives, local(): gathered = lax.all_gather(slip_rates, 'site', axis=1, tiled=True)  16.7 us
    dot_general x2, matrix products, accumulate(): jnp.einsum('pvq,pcqt->vct', slip_block[..., :half_len], band_rows[..., ha...  7.33 us
    dot_general x2, matrix products, accumulate(): jnp.einsum('pvq,pcqt->vct', slip_block[..., half_len:], band_rows[..., :l...  7 us
    slice x2, local copies, waits for them, and re-layouts, band_matrix(): repeated[..., :half_len * (period - 1)]  5.84 us
    all_to_all x1, starting transfers between devices, local(): lax.all_to_all(outgoing, 'patch', split_axis=0, concat_axis=0, tiled=True)  5.17 us
  transfers between devices with their start and end apart: 2, of which 1 were waited for; matrix products, arithmetic and copies ran while one was open for 0% of the time, Pallas kernels for 0%

commit v1 on v0

v1 whole, which is shorter than its diff:
```python
import functools

import jax
import jax.numpy as jnp
from jax import lax
from jax.experimental import pallas as pl
from jax.experimental.pallas import tpu as pltpu
from jax.sharding import PartitionSpec as P

BLOCK = 16
LANES = 128
ROWS = 8
VMEM_LIMIT = 32 * 1024 * 1024


def round_up(value, unit):
    return -(-value // unit) * unit


def params():
    return pltpu.CompilerParams(vmem_limit_bytes=VMEM_LIMIT)


def split_kernel(slip_ref, keep_ref, give_ref):
    patches, both, samples = slip_ref.shape
    rows = both // 2
    per_reg = LANES // BLOCK
    blocks = samples // BLOCK
    core = lax.rem(lax.axis_index("patch"), 2)
    lane_block = lax.broadcasted_iota(jnp.int32, (rows, LANES), 1) // BLOCK
    out_regs = patches * BLOCK // LANES
    for group in range(out_regs):
        done = {}
        for place in range(per_reg):
            full = slip_ref[group * per_reg + place].astype(jnp.float32)
            low, high = full[:rows], full[rows:]
            for which, source in enumerate(
                (jnp.where(core == 0, low, high), jnp.where(core == 0, high, low))
            ):
                for reg in range(samples // LANES):
                    piece = source[:, reg * LANES : (reg + 1) * LANES]
                    for inner in range(per_reg):
                        turn = (place - inner) % per_reg * BLOCK
                        moved = pltpu.roll(piece, turn, 1) if turn else piece
                        key = (which, reg * per_reg + inner)
                        if key in done:
                            done[key] = jnp.where(lane_block == place, moved, done[key])
                        else:
                            done[key] = moved
        for which, ref in enumerate((keep_ref, give_ref)):
            for block in range(0, blocks, 2):
                pair = jnp.concatenate([done[which, block], done[which, block + 1]], axis=0)
                ref[
                    block * rows : (block + 2) * rows, group * LANES : (group + 1) * LANES
                ] = pair.astype(jnp.bfloat16)


def split_slips(slips):
    patches, both, samples = slips.shape
    shape = jax.ShapeDtypeStruct((samples // BLOCK * both // 2, patches * BLOCK), jnp.bfloat16)
    return pl.pallas_call(
        split_kernel, out_shape=(shape, shape), compiler_params=params(), name="split_slips"
    )(slips)


def pick_kernel(slots_ref, *refs):
    pieces, out_ref = refs[:-1], refs[-1]
    own = lax.axis_index("patch")
    width = pieces[0].shape[0]
    count = out_ref.shape[0]
    total = jnp.zeros(out_ref.shape, jnp.float32)
    for step, piece in enumerate(pieces):
        owner = own ^ (2 * step)
        slot = lax.broadcasted_iota(jnp.int32, (count, width), 1) + owner * width
        pick = (slots_ref[...] == slot).astype(jnp.float32).astype(jnp.bfloat16)
        total = total + jnp.dot(pick, piece[...], preferred_element_type=jnp.float32)
    out_ref[...] = total.astype(jnp.bfloat16)


def pick_tiles(slots, pieces):
    shape = jax.ShapeDtypeStruct((slots.shape[0], pieces[0].shape[1]), jnp.bfloat16)
    return pl.pallas_call(
        pick_kernel, out_shape=shape, compiler_params=params(), name="pick_tiles"
    )(slots, *pieces)


def shift_kernel(lags, left_ref, right_ref, out_ref):
    tiles = left_ref[...].astype(jnp.float32) + right_ref[...].astype(jnp.float32)
    count = tiles.shape[0]
    components = tiles.shape[1] // lags
    width = out_ref.shape[1] // components
    tail = jnp.zeros((BLOCK, width - lags), jnp.float32)
    for patch in range(count):
        for comp in range(components):
            row = tiles[patch : patch + 1, comp * lags : (comp + 1) * lags]
            wide = jnp.concatenate([jnp.broadcast_to(row, (BLOCK, lags)), tail], axis=1)
            moved = pltpu.roll(wide, 0, 1, stride=1, stride_axis=0)
            out_ref[
                patch * BLOCK : (patch + 1) * BLOCK, comp * width : (comp + 1) * width
            ] = moved.astype(jnp.bfloat16)


def shift_tiles(left, right, lags):
    components = left.shape[1] // lags
    width = round_up(lags + BLOCK, LANES)
    shape = jax.ShapeDtypeStruct((left.shape[0] * BLOCK, components * width), jnp.bfloat16)
    return pl.pallas_call(
        functools.partial(shift_kernel, lags),
        out_shape=shape,
        compiler_params=params(),
        name="shift_tiles",
    )(left, right)


def convolve_kernel(sites, rows, length, shifted_ref, *refs):
    slip_refs, out_refs = refs[: 2 * sites], refs[2 * sites : 3 * sites]
    stack_ref, product_ref = refs[3 * sites :]
    components = out_refs[0].shape[1]
    height, depth = slip_refs[0].shape
    width = shifted_ref.shape[1] // components
    per_reg = LANES // BLOCK
    blocks = height // rows
    turn = lax.axis_index("site") ^ (lax.axis_index("patch") // 2)
    for step in range(sites):
        place = step ^ turn
        stack_ref[place, :, :depth] = slip_refs[2 * step][...]
        stack_ref[place, :, depth:] = slip_refs[2 * step + 1][...]
    for comp in range(components):
        product_ref[...] = jnp.dot(
            stack_ref[...].reshape(sites * height, 2 * depth),
            shifted_ref[:, comp * width : (comp + 1) * width],
            preferred_element_type=jnp.float32,
        )
        for step in range(sites):
            total = None
            for inner in range(per_reg):
                part = None
                for outer in range(inner, blocks, per_reg):
                    lead = outer // per_reg * LANES
                    start = step * height + outer * rows
                    block = product_ref[start : start + rows, :]
                    pieces = [jnp.zeros((rows, lead), jnp.float32)] if lead else []
                    pieces.append(block[:, : min(width, length - lead)])
                    if length > lead + width:
                        pieces.append(jnp.zeros((rows, length - lead - width), jnp.float32))
                    block = jnp.concatenate(pieces, axis=1) if len(pieces) > 1 else pieces[0]
                    part = block if part is None else part + block
                if inner:
                    part = pltpu.roll(part, inner * BLOCK, 1)
                total = part if total is None else total + part
            out_refs[step][:, comp, :] = total


def convolve(shifted, slips, sites, rows, components, length):
    height, depth = slips[0].shape
    width = shifted.shape[1] // components
    shape = jax.ShapeDtypeStruct((rows, components, length), jnp.float32)
    return pl.pallas_call(
        functools.partial(convolve_kernel, sites, rows, length),
        out_shape=(shape,) * sites,
        scratch_shapes=[
            pltpu.VMEM((sites, height, 2 * depth), jnp.bfloat16),
            pltpu.VMEM((sites * height, width), jnp.float32),
        ],
        compiler_params=params(),
        name="convolve",
    )(shifted, *slips)


def local(slip_rates, green_tiles, patch_slot):
    devices = lax.axis_size("patch")
    sites = lax.axis_size("site")
    chips = devices // 2
    patches, held, samples = slip_rates.shape
    slot_width, components, lags = green_tiles.shape[1:]
    length = samples + lags
    part = held // 2
    rows = round_up(part, ROWS)
    assert chips == sites

    def over_patch(value, offset):
        return lax.ppermute(value, "patch", [(i, i ^ offset) for i in range(devices)])

    def over_site(value, offset):
        return lax.ppermute(value, "site", [(i, i ^ offset) for i in range(sites)])

    slips = slip_rates.reshape(patches, 2, part, samples)
    slips = jnp.pad(slips, ((0, 0), (0, 0), (0, rows - part), (0, 0)))
    keep, give = split_slips(slips.reshape(patches, 2 * rows, samples))
    other = over_patch(give, 1)
    gathered = [keep, other]
    for step in range(1, sites):
        gathered += [over_site(keep, step), over_site(other, step)]

    resident = green_tiles[0].reshape(slot_width, components * lags)
    pieces = [resident] + [over_patch(resident, 2 * step) for step in range(1, chips)]
    own = lax.axis_index("patch")
    by_device = patch_slot.reshape(devices, patches)
    mine = lax.dynamic_index_in_dim(by_device, own, 0, keepdims=False)
    theirs = lax.dynamic_index_in_dim(by_device, own ^ 1, 0, keepdims=False)
    mine, theirs = mine.reshape(-1, 1), theirs.reshape(-1, 1)
    picked = pick_tiles(jnp.concatenate([mine, theirs], axis=0), pieces)
    swapped = jnp.concatenate([picked[patches:], picked[:patches]], axis=0)
    shifted = shift_tiles(picked, over_patch(swapped, 1), lags)

    sums = convolve(shifted, gathered, sites, rows, components, length)
    result = sums[0]
    for step in range(1, chips):
        result = result + over_patch(sums[step], 2 * step)
    return result[None, :part]


def solution(mesh):
    in_specs = (P("patch", "site", None), P("site", "patch", None, None), P())
    out_specs = P("site", "patch", None, None)
    return jax.shard_map(local, mesh=mesh, in_specs=in_specs, out_specs=out_specs, check_vma=False)
```

time: 148 us -> 39 us (0.26)
  waiting for transfers between devices: 55.6 us -> 12.6 us
  local copies, waits for them, and re-layouts: 39.3 us -> 2.67 us
  blocking collectives: 16.7 us -> 0 us
  matrix products: 15 us -> 0 us
  starting transfers between devices: 5.21 us -> 19.7 us
  between operations: 14.1 us -> 0.09 us
  Pallas kernels: 0 us -> 2.9 us
    unnamed x2 -> x0, waiting for transfers between devices: 55.6 us -> none
    reshape x5 -> x2, local copies, waits for them, and re-layouts: 28.1 us -> 0.74 us  [the longest x1 0.73 us: local(): by_device = patch_slot.reshape(devices, patches)]
    ppermute x0 -> x14, starting transfers between devices: none -> 19.7 us  [the longest x6 11 us: over_site(): return lax.ppermute(value, 'site', [(i, i ^ offset) for i in range(sites)])]
    all_gather x1 -> x0, blocking collectives: 16.7 us -> none  [local(): gathered = lax.all_gather(slip_rates, 'site', axis=1, tiled=True)]
    dot_general x6 -> x0, matrix products: 15 us -> none  [the longest x2 7.33 us: accumulate(): jnp.einsum('pvq,pcqt->vct', slip_block[..., :half_len], band_rows[..., ha...]
    ppermute x0 -> x14, waiting for transfers between devices: none -> 12.6 us  [the longest x8 9.11 us: over_patch(): lax.ppermute(value, 'patch', [(i, i ^ offset) for i in range(devices)])]
    slice x2 -> x1, local copies, waits for them, and re-layouts: 5.84 us -> 0.01 us  [local(): swapped = jnp.concatenate([picked[patches:], picked[:patches]], axis=0)]
    all_to_all x1 -> x0, starting transfers between devices: 5.17 us -> none  [local(): lax.all_to_all(outgoing, 'patch', split_axis=0, concat_axis=0, tiled=True)]
  transfers between devices with their start and end apart: 2 -> 14, of which waited for: 1 -> 8; matrix products, arithmetic and copies ran while one was open for 0% -> 2% of each run, Pallas kernels for 0% -> 2%
where the time goes in v1:
time: 39 us; the launch traced here: 38.8 us
  starting transfers between devices  19.7 us (51%)
  waiting for transfers between devices  12.6 us (32%)
  Pallas kernels  2.9 us (7%)
  local copies, waits for them, and re-layouts  2.67 us (7%)
  other arithmetic  0.82 us (2%)
    ppermute x6, starting transfers between devices, over_site(): return lax.ppermute(value, 'site', [(i, i ^ offset) for i in range(sites)])  11 us
    ppermute x8, waiting for transfers between devices, over_patch(): lax.ppermute(value, 'patch', [(i, i ^ offset) for i in range(devices)])  9.11 us
    ppermute x8, starting transfers between devices, over_patch(): lax.ppermute(value, 'patch', [(i, i ^ offset) for i in range(devices)])  8.78 us
    ppermute x6, waiting for transfers between devices, over_site(): return lax.ppermute(value, 'site', [(i, i ^ offset) for i in range(sites)])  3.49 us
    unnamed x3, local copies, waits for them, and re-layouts  1.83 us
    pallas_call x1, Pallas kernels, convolve(): pl.pallas_call(functools.partial(convolve_kernel, sites, rows, length), o...  1.64 us
  transfers between devices with their start and end apart: 14, of which 8 were waited for; matrix products, arithmetic and copies ran while one was open for 2% of the time, Pallas kernels for 2%

profile of v1, /device:TPU:0, one launch (start us, length us, event | category | flops | bytes accessed | tf_op | source)
XLA Modules:
  0.0 38.8 jit_solution(812820272187104185)
XLA Ops:
  0.0 0.9 %copy.7 = bf16[4,8,2,1024]{3,1,2,0:T(8,128)(2,1)S(1)} copy(bf16[4,8,2,1024]{3,2,1,0:T(2,128)(2,1)} %bitcast.13) | data formatting | bytes 262144
  0.9 4.0 %collective-permute-start.2 = (bf16[32,2048]{1,0:T(8,128)(2,1)S(1)}, bf16[32,2048]{1,0:T(8,128)(2,1)S(1)}, u32[]{:S(2)}, u32[]{:S(2)}) collective-permute-start(bf16[32,2048]{1,0:T(8,128)(2,1)S(1)} %bitcast.9), channel_id=1, source_target_pairs={{0,6},{1,7},{2,4},{3,5},{4,2},{5,3},{6,0},{7,1},{8,14},{9,15},{10,... | collective-permute-start | bytes 393224 | tf_op jit(solution)/shard_map/ppermute | solution.py:182
  4.9 0.5 %collective-permute-start.1 = (bf16[32,2048]{1,0:T(8,128)(2,1)S(1)}, bf16[32,2048]{1,0:T(8,128)(2,1)S(1)}, u32[]{:S(2)}, u32[]{:S(2)}) collective-permute-start(bf16[32,2048]{1,0:T(8,128)(2,1)S(1)} %bitcast.10), channel_id=1, source_target_pairs={{0,4},{1,5},{2,6},{3,7},{4,0},{5,1},{6,2},{7,3},{8,12},{9,13},{10,... | collective-permute-start | bytes 393224 | tf_op jit(solution)/shard_map/ppermute | solution.py:182
  5.4 0.1 collective-permute-start
  5.5 0.7 %reshape.13 = s32[8,16]{1,0:T(8,128)S(1)} reshape(s32[128]{0:T(128)} %param.5) | data formatting | bytes 1024 | tf_op jit(solution)/shard_map/reshape | solution.py:198
  6.3 0.1 pad_add_fusion
  6.4 0.1 copy.6.slots_ref
  6.4 2.4 %collective-permute-done.2.refs_3_ = bf16[32,2048]{1,0:T(8,128)(2,1)S(1)} collective-permute-done((bf16[32,2048]{1,0:T(8,128)(2,1)S(1)}, bf16[32,2048]{1,0:T(8,128)(2,1)S(1)}, u32[]{:S(2)}, u32[]{:S(2)}) %collective-permute-start.2) | collective-permute-done | bytes 131104 | tf_op jit(solution)/shard_map/ppermute | solution.py:182
  8.8 2.4 %collective-permute-done.1.refs_2_ = bf16[32,2048]{1,0:T(8,128)(2,1)S(1)} collective-permute-done((bf16[32,2048]{1,0:T(8,128)(2,1)S(1)}, bf16[32,2048]{1,0:T(8,128)(2,1)S(1)}, u32[]{:S(2)}, u32[]{:S(2)}) %collective-permute-start.1) | collective-permute-done | bytes 131104 | tf_op jit(solution)/shard_map/ppermute | solution.py:182
  11.2 0.2 collective-permute-done.refs_1_
  11.4 0.3 pick_tiles.1.left_ref
  11.8 0.1 collective-permute-start.3
  11.9 0.0 copy-start
  11.9 0.9 %copy-done = bf16[16,16,256]{2,1,0:T(8,128)(2,1)S(1)} copy-done((bf16[16,16,256]{2,1,0:T(8,128)(2,1)S(1)}, bf16[16,16,256]{2,1,0:T(8,128)(2,1)}, u32[]{:S(2)}) %copy-start) | copy-done | bytes 131096
  12.8 0.3 split_slips.1
  13.1 0.6 %collective-permute-start.4 = (bf16[128,256]{1,0:T(8,128)(2,1)S(1)}, bf16[128,256]{1,0:T(8,128)(2,1)S(1)}, u32[]{:S(2)}, u32[]{:S(2)}) collective-permute-start(bf16[128,256]{1,0:T(8,128)(2,1)S(1)} %get-tuple-element.12), channel_id=1, source_target_pairs={{0,1},{1,0},{2,3},{3,2},{4,5},{5,4},{6,7},{7,6},{8,9},{9,8},{10,11... | collective-permute-start | bytes 196616 | tf_op jit(solution)/shard_map/ppermute | solution.py:182
  13.7 3.6 %collective-permute-start.9 = (bf16[128,256]{1,0:T(8,128)(2,1)S(1)}, bf16[128,256]{1,0:T(8,128)(2,1)S(1)}, u32[]{:S(2)}, u32[]{:S(2)}) collective-permute-start(bf16[128,256]{1,0:T(8,128)(2,1)S(1)} %get-tuple-element.11.refs_0_), channel_id=1, source_target_pairs={{0,24},{8,16},{16,8},{24,0},{1,25},{9,17},{17,9},{25,1},{2,26},{10... | collective-permute-start | bytes 196616 | tf_op jit(solution)/shard_map/ppermute | solution.py:185
  17.3 0.8 %collective-permute-start.5 = (bf16[128,256]{1,0:T(8,128)(2,1)S(1)}, bf16[128,256]{1,0:T(8,128)(2,1)S(1)}, u32[]{:S(2)}, u32[]{:S(2)}) collective-permute-start(bf16[128,256]{1,0:T(8,128)(2,1)S(1)} %get-tuple-element.11.refs_0_), channel_id=1, source_target_pairs={{0,8},{8,0},{16,24},{24,16},{1,9},{9,1},{17,25},{25,17},{2,10},{10... | collective-permute-start | bytes 196616 | tf_op jit(solution)/shard_map/ppermute | solution.py:185
  18.1 3.6 %collective-permute-start.10 = (bf16[128,256]{1,0:T(8,128)(2,1)S(1)}, bf16[128,256]{1,0:T(8,128)(2,1)S(1)}, u32[]{:S(2)}, u32[]{:S(2)}) collective-permute-start(bf16[128,256]{1,0:T(8,128)(2,1)S(1)} %collective-permute-done.4.refs_1_), channel_id=1, source_target_pairs={{0,24},{8,16},{16,8},{24,0},{1,25},{9,17},{17,9},{25,1},{2,26},{10... | collective-permute-start | bytes 196616 | tf_op jit(solution)/shard_map/ppermute | solution.py:185
  21.7 1.5 %collective-permute-start.8 = (bf16[128,256]{1,0:T(8,128)(2,1)S(1)}, bf16[128,256]{1,0:T(8,128)(2,1)S(1)}, u32[]{:S(2)}, u32[]{:S(2)}) collective-permute-start(bf16[128,256]{1,0:T(8,128)(2,1)S(1)} %collective-permute-done.4.refs_1_), channel_id=1, source_target_pairs={{0,16},{8,24},{16,0},{24,8},{1,17},{9,25},{17,1},{25,9},{2,18},{10... | collective-permute-start | bytes 196616 | tf_op jit(solution)/shard_map/ppermute | solution.py:185
  23.2 1.5 %collective-permute-start.6 = (bf16[128,256]{1,0:T(8,128)(2,1)S(1)}, bf16[128,256]{1,0:T(8,128)(2,1)S(1)}, u32[]{:S(2)}, u32[]{:S(2)}) collective-permute-start(bf16[128,256]{1,0:T(8,128)(2,1)S(1)} %collective-permute-done.4.refs_1_), channel_id=1, source_target_pairs={{0,8},{8,0},{16,24},{24,16},{1,9},{9,1},{17,25},{25,17},{2,10},{10... | collective-permute-start | bytes 196616 | tf_op jit(solution)/shard_map/ppermute | solution.py:185
  24.7 0.6 %shift_tiles.1.shifted_ref = bf16[512,2304]{1,0:T(8,128)(2,1)S(1)} custom-call(bf16[32,2048]{1,0:T(8,128)(2,1)S(1)} %pick_tiles.1.left_ref, bf16[32,2048]{1,0:T(8,128)(2,1)S(1)} %collective-permute-done.3.right_ref), custom_call_target="tpu_custom_call" | custom-call | tf_op jit(solution)/shard_map/shift_tiles/pallas_call | solution.py:107
  25.3 0.4 %collective-permute-done.7.refs_4_ = bf16[128,256]{1,0:T(8,128)(2,1)S(1)} collective-permute-done((bf16[128,256]{1,0:T(8,128)(2,1)S(1)}, bf16[128,256]{1,0:T(8,128)(2,1)S(1)}, u32[]{:S(2)}, u32[]{:S(2)}) %collective-permute-start.7) | collective-permute-done | bytes 65568 | tf_op jit(solution)/shard_map/ppermute | solution.py:185
  25.7 3.1 %collective-permute-done.8.refs_5_ = bf16[128,256]{1,0:T(8,128)(2,1)S(1)} collective-permute-done((bf16[128,256]{1,0:T(8,128)(2,1)S(1)}, bf16[128,256]{1,0:T(8,128)(2,1)S(1)}, u32[]{:S(2)}, u32[]{:S(2)}) %collective-permute-start.8) | collective-permute-done | bytes 65568 | tf_op jit(solution)/shard_map/ppermute | solution.py:185
  28.8 1.6 %convolve.1 = (f32[8,2,1280]{2,1,0:T(2,128)S(1)}, f32[8,2,1280]{2,1,0:T(2,128)S(1)}, f32[8,2,1280]{2,1,0:T(2,128)S(1)}, f32[8,2,1280]{2,1,0:T(2,128)S(1)}) custom-call(bf16[512,2304]{1,0:T(8,128)(2,1)S(1)} %shift_tiles.1.shifted_ref, bf16[128,256]{1,0:T(8,128)(2,1)S(1)} %get-tuple-element.11.refs_0_, bf16[128,256]{1,0:T(8,128)(2,1)S(1)} %collective-permute-done.4.refs_1_, ...), custom_call_target="tpu_custom_call" | custom-call | tf_op jit(solution)/shard_map/convolve/pallas_call | solution.py:158
  30.4 1.6 %collective-permute-start.11 = (f32[8,2,1280]{2,1,0:T(2,128)S(1)}, f32[8,2,1280]{2,1,0:T(2,128)S(1)}, u32[]{:S(2)}, u32[]{:S(2)}) collective-permute-start(f32[8,2,1280]{2,1,0:T(2,128)S(1)} %get-tuple-element.14), channel_id=1, source_target_pairs={{0,2},{1,3},{2,0},{3,1},{4,6},{5,7},{6,4},{7,5},{8,10},{9,11},{10,... | collective-permute-start | bytes 245768 | tf_op jit(solution)/shard_map/ppermute | solution.py:182
  32.0 0.7 %collective-permute-start.12 = (f32[8,2,1280]{2,1,0:T(2,128)S(1)}, f32[8,2,1280]{2,1,0:T(2,128)S(1)}, u32[]{:S(2)}, u32[]{:S(2)}) collective-permute-start(f32[8,2,1280]{2,1,0:T(2,128)S(1)} %get-tuple-element.15), channel_id=1, source_target_pairs={{0,4},{1,5},{2,6},{3,7},{4,0},{5,1},{6,2},{7,3},{8,12},{9,13},{10,... | collective-permute-start | bytes 245768 | tf_op jit(solution)/shard_map/ppermute | solution.py:182
  32.7 1.2 %collective-permute-start.13 = (f32[8,2,1280]{2,1,0:T(2,128)S(1)}, f32[8,2,1280]{2,1,0:T(2,128)S(1)}, u32[]{:S(2)}, u32[]{:S(2)}) collective-permute-start(f32[8,2,1280]{2,1,0:T(2,128)S(1)} %get-tuple-element.16), channel_id=1, source_target_pairs={{0,6},{1,7},{2,4},{3,5},{4,2},{5,3},{6,0},{7,1},{8,14},{9,15},{10,... | collective-permute-start | bytes 245768 | tf_op jit(solution)/shard_map/ppermute | solution.py:182
  34.0 1.0 %collective-permute-done.11 = f32[8,2,1280]{2,1,0:T(2,128)S(1)} collective-permute-done((f32[8,2,1280]{2,1,0:T(2,128)S(1)}, f32[8,2,1280]{2,1,0:T(2,128)S(1)}, u32[]{:S(2)}, u32[]{:S(2)}) %collective-permute-start.11) | collective-permute-done | bytes 81952 | tf_op jit(solution)/shard_map/ppermute | solution.py:182
  34.9 2.2 %collective-permute-done.12 = f32[8,2,1280]{2,1,0:T(2,128)S(1)} collective-permute-done((f32[8,2,1280]{2,1,0:T(2,128)S(1)}, f32[8,2,1280]{2,1,0:T(2,128)S(1)}, u32[]{:S(2)}, u32[]{:S(2)}) %collective-permute-start.12) | collective-permute-done | bytes 81952 | tf_op jit(solution)/shard_map/ppermute | solution.py:182
  37.2 0.9 %collective-permute-done.13 = f32[8,2,1280]{2,1,0:T(2,128)S(1)} collective-permute-done((f32[8,2,1280]{2,1,0:T(2,128)S(1)}, f32[8,2,1280]{2,1,0:T(2,128)S(1)}, u32[]{:S(2)}, u32[]{:S(2)}) %collective-permute-start.13) | collective-permute-done | bytes 81952 | tf_op jit(solution)/shard_map/ppermute | solution.py:182
  38.1 0.7 %add_bitcast_fusion = f32[1,8,2,1280]{3,2,1,0:T(2,128)} fusion(f32[8,2,1280]{2,1,0:T(2,128)S(1)} %collective-permute-done.13, f32[8,2,1280]{2,1,0:T(2,128)S(1)} %collective-permute-done.12, f32[8,2,1280]{2,1,0:T(2,128)S(1)} %get-tuple-element.13, f32[8,2,1280]{2,1,0:T(2,128)S(1)} %collective-permute-done.11), kind=kLoop, calls=%fused_computation.1 | loop fusion | flops 61440 | bytes 409600 | tf_op jit(solution)/shard_map/broadcast_in_dim | solution.py:210
  (10 shorter events, 0.0 us)
Async XLA Ops:
  0.9 7.9 %collective-permute-start.2 = (bf16[32,2048]{1,0:T(8,128)(2,1)S(1)}, bf16[32,2048]{1,0:T(8,128)(2,1)S(1)}, u32[]{:S(2)}, u32[]{:S(2)}) collective-permute-start(bf16[32,2048]{1,0:T(8,128)(2,1)S(1)} %bitcast.9), channel_id=1, source_target_pairs={{0,6},{1,7},{2,4},{3,5},{4,2},{5,3},{6,0},{7,1},{8,14},{9,15},{10,... | collective-permute-start | bytes 393224 | tf_op jit(solution)/shard_map/ppermute | solution.py:182
  4.9 6.3 %collective-permute-start.1 = (bf16[32,2048]{1,0:T(8,128)(2,1)S(1)}, bf16[32,2048]{1,0:T(8,128)(2,1)S(1)}, u32[]{:S(2)}, u32[]{:S(2)}) collective-permute-start(bf16[32,2048]{1,0:T(8,128)(2,1)S(1)} %bitcast.10), channel_id=1, source_target_pairs={{0,4},{1,5},{2,6},{3,7},{4,0},{5,1},{6,2},{7,3},{8,12},{9,13},{10,... | collective-permute-start | bytes 393224 | tf_op jit(solution)/shard_map/ppermute | solution.py:182
  5.4 6.0 %collective-permute-start = (bf16[32,2048]{1,0:T(8,128)(2,1)S(1)}, bf16[32,2048]{1,0:T(8,128)(2,1)S(1)}, u32[]{:S(2)}, u32[]{:S(2)}) collective-permute-start(bf16[32,2048]{1,0:T(8,128)(2,1)S(1)} %bitcast.11), channel_id=1, source_target_pairs={{0,2},{1,3},{2,0},{3,1},{4,6},{5,7},{6,4},{7,5},{8,10},{9,11},{10,... | collective-permute-start | bytes 393224 | tf_op jit(solution)/shard_map/ppermute | solution.py:182
  11.8 11.3 %collective-permute-start.3 = (bf16[32,2048]{1,0:T(8,128)(2,1)S(1)}, bf16[32,2048]{1,0:T(8,128)(2,1)S(1)}, u32[]{:S(2)}, u32[]{:S(2)}) collective-permute-start(bf16[32,2048]{1,0:T(8,128)(2,1)S(1)} %pad_maximum_fusion), channel_id=1, source_target_pairs={{0,1},{1,0},{2,3},{3,2},{4,5},{5,4},{6,7},{7,6},{8,9},{9,8},{10,11... | collective-permute-start | bytes 393224 | tf_op jit(solution)/shard_map/ppermute | solution.py:182
  11.9 0.9 %copy-start = (bf16[16,16,256]{2,1,0:T(8,128)(2,1)S(1)}, bf16[16,16,256]{2,1,0:T(8,128)(2,1)}, u32[]{:S(2)}) copy-start(bf16[16,16,256]{2,1,0:T(8,128)(2,1)} %slip_ref.1) | copy-start | bytes 393220
  13.1 5.0 %collective-permute-start.4 = (bf16[128,256]{1,0:T(8,128)(2,1)S(1)}, bf16[128,256]{1,0:T(8,128)(2,1)S(1)}, u32[]{:S(2)}, u32[]{:S(2)}) collective-permute-start(bf16[128,256]{1,0:T(8,128)(2,1)S(1)} %get-tuple-element.12), channel_id=1, source_target_pairs={{0,1},{1,0},{2,3},{3,2},{4,5},{5,4},{6,7},{7,6},{8,9},{9,8},{10,11... | collective-permute-start | bytes 196616 | tf_op jit(solution)/shard_map/ppermute | solution.py:182
  13.7 8.0 %collective-permute-start.9 = (bf16[128,256]{1,0:T(8,128)(2,1)S(1)}, bf16[128,256]{1,0:T(8,128)(2,1)S(1)}, u32[]{:S(2)}, u32[]{:S(2)}) collective-permute-start(bf16[128,256]{1,0:T(8,128)(2,1)S(1)} %get-tuple-element.11.refs_0_), channel_id=1, source_target_pairs={{0,24},{8,16},{16,8},{24,0},{1,25},{9,17},{17,9},{25,1},{2,26},{10... | collective-permute-start | bytes 196616 | tf_op jit(solution)/shard_map/ppermute | solution.py:185
  17.3 8.4 %collective-permute-start.7 = (bf16[128,256]{1,0:T(8,128)(2,1)S(1)}, bf16[128,256]{1,0:T(8,128)(2,1)S(1)}, u32[]{:S(2)}, u32[]{:S(2)}) collective-permute-start(bf16[128,256]{1,0:T(8,128)(2,1)S(1)} %get-tuple-element.11.refs_0_), channel_id=1, source_target_pairs={{0,16},{8,24},{16,0},{24,8},{1,17},{9,25},{17,1},{25,9},{2,18},{10... | collective-permute-start | bytes 196616 | tf_op jit(solution)/shard_map/ppermute | solution.py:185
  17.3 8.4 %collective-permute-start.5 = (bf16[128,256]{1,0:T(8,128)(2,1)S(1)}, bf16[128,256]{1,0:T(8,128)(2,1)S(1)}, u32[]{:S(2)}, u32[]{:S(2)}) collective-permute-start(bf16[128,256]{1,0:T(8,128)(2,1)S(1)} %get-tuple-element.11.refs_0_), channel_id=1, source_target_pairs={{0,8},{8,0},{16,24},{24,16},{1,9},{9,1},{17,25},{25,17},{2,10},{10... | collective-permute-start | bytes 196616 | tf_op jit(solution)/shard_map/ppermute | solution.py:185
  18.1 7.6 %collective-permute-start.10 = (bf16[128,256]{1,0:T(8,128)(2,1)S(1)}, bf16[128,256]{1,0:T(8,128)(2,1)S(1)}, u32[]{:S(2)}, u32[]{:S(2)}) collective-permute-start(bf16[128,256]{1,0:T(8,128)(2,1)S(1)} %collective-permute-done.4.refs_1_), channel_id=1, source_target_pairs={{0,24},{8,16},{16,8},{24,0},{1,25},{9,17},{17,9},{25,1},{2,26},{10... | collective-permute-start | bytes 196616 | tf_op jit(solution)/shard_map/ppermute | solution.py:185
  21.7 7.1 %collective-permute-start.8 = (bf16[128,256]{1,0:T(8,128)(2,1)S(1)}, bf16[128,256]{1,0:T(8,128)(2,1)S(1)}, u32[]{:S(2)}, u32[]{:S(2)}) collective-permute-start(bf16[128,256]{1,0:T(8,128)(2,1)S(1)} %collective-permute-done.4.refs_1_), channel_id=1, source_target_pairs={{0,16},{8,24},{16,0},{24,8},{1,17},{9,25},{17,1},{25,9},{2,18},{10... | collective-permute-start | bytes 196616 | tf_op jit(solution)/shard_map/ppermute | solution.py:185
  23.2 5.6 %collective-permute-start.6 = (bf16[128,256]{1,0:T(8,128)(2,1)S(1)}, bf16[128,256]{1,0:T(8,128)(2,1)S(1)}, u32[]{:S(2)}, u32[]{:S(2)}) collective-permute-start(bf16[128,256]{1,0:T(8,128)(2,1)S(1)} %collective-permute-done.4.refs_1_), channel_id=1, source_target_pairs={{0,8},{8,0},{16,24},{24,16},{1,9},{9,1},{17,25},{25,17},{2,10},{10... | collective-permute-start | bytes 196616 | tf_op jit(solution)/shard_map/ppermute | solution.py:185
  30.4 4.5 %collective-permute-start.11 = (f32[8,2,1280]{2,1,0:T(2,128)S(1)}, f32[8,2,1280]{2,1,0:T(2,128)S(1)}, u32[]{:S(2)}, u32[]{:S(2)}) collective-permute-start(f32[8,2,1280]{2,1,0:T(2,128)S(1)} %get-tuple-element.14), channel_id=1, source_target_pairs={{0,2},{1,3},{2,0},{3,1},{4,6},{5,7},{6,4},{7,5},{8,10},{9,11},{10,... | collective-permute-start | bytes 245768 | tf_op jit(solution)/shard_map/ppermute | solution.py:182
  32.0 5.2 %collective-permute-start.12 = (f32[8,2,1280]{2,1,0:T(2,128)S(1)}, f32[8,2,1280]{2,1,0:T(2,128)S(1)}, u32[]{:S(2)}, u32[]{:S(2)}) collective-permute-start(f32[8,2,1280]{2,1,0:T(2,128)S(1)} %get-tuple-element.15), channel_id=1, source_target_pairs={{0,4},{1,5},{2,6},{3,7},{4,0},{5,1},{6,2},{7,3},{8,12},{9,13},{10,... | collective-permute-start | bytes 245768 | tf_op jit(solution)/shard_map/ppermute | solution.py:182
  32.7 5.3 %collective-permute-start.13 = (f32[8,2,1280]{2,1,0:T(2,128)S(1)}, f32[8,2,1280]{2,1,0:T(2,128)S(1)}, u32[]{:S(2)}, u32[]{:S(2)}) collective-permute-start(f32[8,2,1280]{2,1,0:T(2,128)S(1)} %get-tuple-element.16), channel_id=1, source_target_pairs={{0,6},{1,7},{2,4},{3,5},{4,2},{5,3},{6,0},{7,1},{8,14},{9,15},{10,... | collective-permute-start | bytes 245768 | tf_op jit(solution)/shard_map/ppermute | solution.py:182
